TPU v7x, 32 devices: a whole 2x2x4 slice. The times are simulated.
32 devices in a mesh: grp: 2 (over y), pts: 8 (over z, x), ctr: 2 (over core).
Axes of the slice: x: 2, y: 2, z: 4, core: 2. Of those that a mesh axis runs over, the one named last changes fastest.
Arguments:
- points: bfloat16 [3072, 128], P(('grp', 'pts')), parts along dimension 0, may hold values from -1.5 to 1.5
- curvature: bfloat16 [3072, 32], P(('grp', 'pts')), parts along dimension 0, may hold values from 0.019897461 to 0.25
- centers: bfloat16 [128, 131072], P(None, ('grp', 'pts', 'ctr')), parts along dimension 1, may hold values from -1.5 to 1.5
- coef: bfloat16 [32, 131072], P(None, ('grp', 'pts', 'ctr')), parts along dimension 1, may hold values from -1.1953125 to 1.1953125
Outputs:
- hvp: float32 [32, 131072], P(None, ('grp', 'pts', 'ctr')), parts along dimension 1
There are 2 independent parts, one for each index of `grp`. A program takes and returns all parts, laid end to end along the dimension named above; each array names one. Nothing has to cross between parts.
All inputs are finite; a program needn't handle non-finite values.
Results may differ from a plain program's by a relative error of at most 0.0003.
Values may be sent and summed in bfloat16 or wider, within the bound.
A program may use at most 64 MiB of HBM per device.

v0:
```python
import jax
import jax.numpy as jnp
from jax import lax
from jax.sharding import PartitionSpec as P


def kernel_tile(points, sq_points, block, scale):
    sq_centers = jnp.sum(jnp.square(block.astype(jnp.float32)), axis=0)
    inner = jnp.dot(points, block, preferred_element_type=jnp.float32)
    dist = sq_points[:, None] + sq_centers[None, :] - 2.0 * inner
    return jnp.exp(-dist * scale).astype(jnp.bfloat16)


def on_device(points, curvature, centers, coef):
    scale = 32.0 / points.shape[1]
    labels = coef.shape[0]
    near_centers, near_coef = (
        lax.all_gather(centers, "pts", axis=1, tiled=True),
        lax.all_gather(coef, "pts", axis=1, tiled=True),
    )
    total = near_centers.shape[1]
    width = total // 4
    sq_points = jnp.sum(jnp.square(points.astype(jnp.float32)), axis=1)
    tangent = jnp.zeros((points.shape[0], labels), jnp.float32)
    for number in range(4):
        block = near_centers[:, number * width : (number + 1) * width]
        tile = kernel_tile(points, sq_points, block, scale)
        values = near_coef[:, number * width : (number + 1) * width]
        tangent = tangent + lax.dot_general(
            tile, values, (((1,), (1,)), ((), ())), preferred_element_type=jnp.float32
        )
    tangent = lax.psum(tangent, "ctr")
    weighted = (curvature.astype(jnp.float32) * tangent).astype(jnp.bfloat16)
    pieces = []
    for number in range(4):
        block = near_centers[:, number * width : (number + 1) * width]
        tile = kernel_tile(points, sq_points, block, scale)
        pieces.append(
            lax.dot_general(
                weighted, tile, (((0,), (0,)), ((), ())), preferred_element_type=jnp.float32
            )
        )
    partial_sum = jnp.concatenate(pieces, axis=1)
    return lax.psum_scatter(partial_sum, "pts", scatter_dimension=1, tiled=True)


def solution(mesh):
    in_specs = (
        P(("grp", "pts"), None),
        P(("grp", "pts"), None),
        P(None, ("grp", "pts", "ctr")),
        P(None, ("grp", "pts", "ctr")),
    )
    out_specs = P(None, ("grp", "pts", "ctr"))
    return jax.shard_map(
        on_device, mesh=mesh, in_specs=in_specs, out_specs=out_specs, check_vma=False
    )
```

profile of v0, /device:TPU:0, one launch (start us, length us, event | category | flops | bytes accessed | tf_op | source)
XLA Modules:
  0.0 299.0 jit_solution(7907585057710424661)
XLA Ops:
  6.5 0.7 all-gather.3.cloned.1.call-update
  7.3 0.7 all-gather.5.cloned.1.call-update
  8.1 0.9 multiply_reduce_fusion.4
  9.0 128.2 %all-gather.3.cloned.1.call-done = bf16[128,32768]{1,0:T(8,128)(2,1)} async-done(((bf16[128,4096]{1,0:T(8,128)(2,1)}), bf16[128,32768]{1,0:T(8,128)(2,1)}) %all-gather.3.cloned.1.call-update) | async-done | bytes 8388624 | tf_op jit(solution)/shard_map/all_gather | solution.py:18
  137.2 4.5 %multiply_reduce_fusion = (f32[8192]{0:T(1024)S(1)}, f32[8192]{0:T(1024)S(1)}, f32[8192]{0:T(1024)S(1)}, f32[8192]{0:T(1024)S(1)}) fusion(bf16[128,32768]{1,0:T(8,128)(2,1)} %all-gather.3.cloned.1.call-done), kind=kLoop, calls=%fused_computation.25 | loop fusion | flops 12550144 | bytes 8519680 | tf_op jit(solution)/shard_map/reduce_sum | solution.py:8
  141.7 1.3 copy-done.4
  143.0 1.8 fusion.19
  144.9 3.5 %fusion.18 = bf16[192,8192]{1,0:T(8,128)(2,1)} fusion(bf16[192,128]{1,0:T(8,128)(2,1)S(1)} %copy-done.6, f32[8192]{0:T(1024)S(1)} %get-tuple-element.6, f32[192]{0:T(256)S(1)} %multiply_reduce_fusion.4, bf16[128,32768]{1,0:T(8,128)(2,1)S(1)} %copy-done.4), kind=kOutput, calls=%fused_computation.22 | convolution fusion | flops 412090368 | bytes 5325824 | tf_op jit(solution)/shard_map/dot_general | solution.py:9
  148.4 3.5 %fusion.17 = bf16[192,8192]{1,0:T(8,128)(2,1)} fusion(bf16[192,128]{1,0:T(8,128)(2,1)S(1)} %copy-done.6, f32[8192]{0:T(1024)S(1)} %get-tuple-element.7, f32[192]{0:T(256)S(1)} %multiply_reduce_fusion.4, bf16[128,32768]{1,0:T(8,128)(2,1)S(1)} %copy-done.4), kind=kOutput, calls=%fused_computation.21 | convolution fusion | flops 412090368 | bytes 5325824 | tf_op jit(solution)/shard_map/dot_general | solution.py:9
  151.9 3.5 %fusion.16 = bf16[192,8192]{1,0:T(8,128)(2,1)} fusion(bf16[192,128]{1,0:T(8,128)(2,1)S(1)} %copy-done.6, f32[8192]{0:T(1024)S(1)} %get-tuple-element.8, f32[192]{0:T(256)S(1)} %multiply_reduce_fusion.4, bf16[128,32768]{1,0:T(8,128)(2,1)S(1)} %copy-done.4), kind=kOutput, calls=%fused_computation.20 | convolution fusion | flops 412090368 | bytes 5325824 | tf_op jit(solution)/shard_map/dot_general | solution.py:9
  155.4 31.4 %all-gather.5.cloned.1.call-done = bf16[32,32768]{1,0:T(8,128)(2,1)} async-done(((bf16[32,4096]{1,0:T(8,128)(2,1)}), bf16[32,32768]{1,0:T(8,128)(2,1)}) %all-gather.5.cloned.1.call-update) | async-done | bytes 2097168 | tf_op jit(solution)/shard_map/all_gather | solution.py:19
  186.9 3.2 %fusion.27 = f32[192,32]{0,1:T(8,128)S(1)} fusion(bf16[192,8192]{1,0:T(8,128)(2,1)} %fusion.16, bf16[32,32768]{1,0:T(8,128)(2,1)} %all-gather.5.cloned.1.call-done), kind=kOutput, calls=%fused_computation.39 | convolution fusion | flops 100663296 | bytes 3694592 | tf_op jit(solution)/shard_map/dot_general | solution.py:29
  190.1 3.1 %convolution_add_fusion.2 = f32[192,32]{0,1:T(8,128)S(1)} fusion(f32[192,32]{0,1:T(8,128)S(1)} %fusion.27, bf16[192,8192]{1,0:T(8,128)(2,1)} %fusion.17, bf16[32,32768]{1,0:T(8,128)(2,1)} %all-gather.5.cloned.1.call-done), kind=kOutput, calls=%fused_computation.35 | convolution fusion | flops 100669440 | bytes 3719168 | tf_op jit(solution)/shard_map/dot_general | solution.py:29
  193.2 1.1 convolution_add_fusion.1
  194.3 1.1 convolution_add_fusion
  195.3 3.4 %psum.7 = f32[192,32]{0,1:T(8,128)S(1)} all-reduce(f32[192,32]{0,1:T(8,128)S(1)} %convolution_add_fusion), channel_id=1, replica_groups=mesh['grp'=2,'pts'=8,'ctr'=2] {'ctr'}, use_global_device_ids=true, to_apply=%region_5.0 | all-reduce | flops 6144 | bytes 49152 | tf_op jit(solution)/shard_map/psum | solution.py:32
  198.8 0.7 fusion.32
  199.5 1.2 copy-done.1
  200.7 0.7 fusion.31
  201.6 0.7 fusion.30
  202.3 0.5 copy-done.3
  202.8 0.7 fusion.29
  203.5 2.2 pad_maximum_fusion
  205.7 86.8 %reduce-scatter.2.cloned.1.call-done = f32[32,4096]{1,0:T(8,128)} async-done(((f32[32,32768]{1,0:T(8,128)}), f32[32,4096]{1,0:T(8,128)}) %reduce-scatter.2.cloned.1.call-update) | async-done | bytes 524304 | tf_op jit(solution)/shard_map/reduce_scatter | solution.py:44
  (18 shorter events, 0.4 us)
Async XLA Ops:
  6.5 130.6 %all-gather.3.cloned.1.call-start = ((), (), s32[]{:S(2)}) async-start(), calls=%async_computation.1 | async-start | bytes 9437184 | tf_op jit(solution)/shard_map/all_gather | solution.py:18
  7.3 179.6 %all-gather.5.cloned.1.call-start = ((), (), s32[]{:S(2)}) async-start(), calls=%async_computation.2 | async-start | bytes 2359296 | tf_op jit(solution)/shard_map/all_gather | solution.py:19
  8.0 284.5 %reduce-scatter.2.cloned.1.call-start = ((), (), s32[]{:S(2)}) async-start(), calls=%async_computation.3 | async-start | bytes 4718592 | tf_op jit(solution)/shard_map/reduce_scatter | solution.py:44
  9.0 132.7 %copy-start.6 = (bf16[192,128]{1,0:T(8,128)(2,1)S(1)}, bf16[192,128]{1,0:T(8,128)(2,1)}, u32[]{:S(2)}) copy-start(bf16[192,128]{1,0:T(8,128)(2,1)} %param.4) | copy-start | bytes 147460
  137.2 5.9 %copy-start.4 = (bf16[128,32768]{1,0:T(8,128)(2,1)S(1)}, bf16[128,32768]{1,0:T(8,128)(2,1)}, u32[]{:S(2)}) copy-start(bf16[128,32768]{1,0:T(8,128)(2,1)} %all-gather.3.cloned.1.call-done) | copy-start | bytes 25165828
  186.9 6.3 %copy-start = (bf16[192,8192]{1,0:T(8,128)(2,1)S(1)}, bf16[192,8192]{1,0:T(8,128)(2,1)}, u32[]{:S(2)}) copy-start(bf16[192,8192]{1,0:T(8,128)(2,1)} %fusion.18) | copy-start | bytes 9437188
  186.9 6.3 %copy-start.5 = (bf16[32,32768]{1,0:T(8,128)(2,1)S(1)}, bf16[32,32768]{1,0:T(8,128)(2,1)}, u32[]{:S(2)}) copy-start(bf16[32,32768]{1,0:T(8,128)(2,1)} %all-gather.5.cloned.1.call-done) | copy-start | bytes 6291460
  193.2 5.6 %copy-start.7 = (bf16[192,32]{0,1:T(8,128)(2,1)S(1)}, bf16[192,32]{0,1:T(8,128)(2,1)}, u32[]{:S(2)}) copy-start(bf16[192,32]{0,1:T(8,128)(2,1)} %param.5) | copy-start | bytes 36868
  198.8 1.9 copy-start.1
  198.8 2.8 copy-start.2
  200.7 2.1 copy-start.3
Sparse Core Ops, SparseCore 0:
  9.5 127.5 all-gather.2
  139.4 47.4 all-gather.4
  205.8 86.5 reduce-scatter.1
where the time goes:
time: 299 us
  waiting for transfers between devices  248 us (83%)
  matrix products  23.5 us (8%)
  between operations  13.2 us (4%)
  other arithmetic  7.63 us (3%)
  blocking collectives  3.41 us (1%)
  local copies, waits for them, and re-layouts  3.29 us (1%)
    all_gather x1, waiting for transfers between devices, on_device(): lax.all_gather(centers, 'pts', axis=1, tiled=True)  128 us
    reduce_scatter x1, waiting for transfers between devices, on_device(): return lax.psum_scatter(partial_sum, 'pts', scatter_dimension=1, tiled=True)  86.8 us
    all_gather x1, waiting for transfers between devices, on_device(): lax.all_gather(coef, 'pts', axis=1, tiled=True)  31.4 us
    dot_general x4, matrix products, kernel_tile(): inner = jnp.dot(points, block, preferred_element_type=jnp.float32)  12.4 us
    dot_general x4, matrix products, on_device(): lax.dot_general(tile, values, (((1,), (1,)), ((), ())), preferred_element...  8.42 us
  transfers between devices with their start and end apart: 3, of which 3 were waited for; matrix products, arithmetic and copies ran while one was open for 6% of the time, Pallas kernels for 0%

commit v1 on v0

--- a/solution.py
+++ b/solution.py
@@ -2,6 +2,7 @@
 import jax.numpy as jnp
 from jax import lax
 from jax.sharding import PartitionSpec as P
+from jax.lax import axis_index, axis_size, ppermute
 
 
 def kernel_tile(points, sq_points, block, scale):
@@ -12,11 +13,24 @@
 
 
 def on_device(points, curvature, centers, coef):
+
+    def follow_the_entries(ax_name, array_here):
+        dev_n = axis_size(ax_name)
+        series = list(map(lambda d: (d, (d + 1) % dev_n), range(dev_n)))
+        rows = list(map(lambda d: (d, (d - 1) % dev_n), range(dev_n)))
+        mid_arr, front = ([array_here], [array_here])
+        for _ in range(dev_n // 2):
+            mid_arr.append(ppermute(mid_arr[-1], ax_name, series))
+        for _ in [*range((dev_n - 1) // 2)]:
+            front.append(ppermute(front[-1], ax_name, rows))
+        f_next = jnp.concatenate([*mid_arr[::-1], *front[1:]], 1)
+        return jnp.roll(f_next, (axis_index(ax_name) - dev_n // 2) * array_here.shape[1], 1)
+
     scale = 32.0 / points.shape[1]
     labels = coef.shape[0]
     near_centers, near_coef = (
         lax.all_gather(centers, "pts", axis=1, tiled=True),
-        lax.all_gather(coef, "pts", axis=1, tiled=True),
+        follow_the_entries("pts", coef),
     )
     total = near_centers.shape[1]
     width = total // 4

time: 299 us -> 284 us (0.950)
  waiting for transfers between devices: 248 us -> 208 us
  starting transfers between devices: 0.08 us -> 14.3 us
  local copies, waits for them, and re-layouts: 3.29 us -> 14.4 us
    all_gather x1, waiting for transfers between devices: 128 us -> 74.7 us  [on_device(): lax.all_gather(centers, 'pts', axis=1, tiled=True)]
    ppermute x0 -> x7, waiting for transfers between devices: none -> 46.5 us  [the longest x4 42.9 us: follow_the_entries(): mid_arr.append(ppermute(mid_arr[-1], ax_name, series))]
    all_gather x1 -> x0, waiting for transfers between devices: 31.4 us -> none  [on_device(): lax.all_gather(coef, 'pts', axis=1, tiled=True)]
    ppermute x0 -> x7, starting transfers between devices: none -> 14.2 us  [the longest x4 8.54 us: follow_the_entries(): mid_arr.append(ppermute(mid_arr[-1], ax_name, series))]
    unnamed x16 -> x33, local copies, waits for them, and re-layouts: 3.29 us -> 13.7 us
    dot_general x4, matrix products: 12.4 us -> 7.32 us  [kernel_tile(): inner = jnp.dot(points, block, preferred_element_type=jnp.float32)]
  transfers between devices with their start and end apart: 3 -> 9, of which waited for: 3 -> 8; matrix products, arithmetic and copies ran while one was open for 6% -> 5% of each run, Pallas kernels for 0% -> 0%
where the time goes in v1:
time: 284 us; the launch traced here: 283 us
  waiting for transfers between devices  208 us (73%)
  matrix products  21.8 us (8%)
  local copies, waits for them, and re-layouts  14.4 us (5%)
  starting transfers between devices  14.3 us (5%)
  between operations  13.6 us (5%)
  other arithmetic  7.64 us (3%)
  blocking collectives  3.41 us (1%)
    reduce_scatter x1, waiting for transfers between devices, on_device(): return lax.psum_scatter(partial_sum, 'pts', scatter_dimension=1, tiled=True)  86.3 us
    all_gather x1, waiting for transfers between devices, on_device(): lax.all_gather(centers, 'pts', axis=1, tiled=True)  74.7 us
    ppermute x4, waiting for transfers between devices, follow_the_entries(): mid_arr.append(ppermute(mid_arr[-1], ax_name, series))  42.9 us
    unnamed x33, local copies, waits for them, and re-layouts  13.7 us
    dot_general x4, matrix products, on_device(): lax.dot_general(tile, values, (((1,), (1,)), ((), ())), preferred_element...  9.67 us
    ppermute x4, starting transfers between devices, follow_the_entries(): mid_arr.append(ppermute(mid_arr[-1], ax_name, series))  8.54 us
    dot_general x4, matrix products, kernel_tile(): inner = jnp.dot(points, block, preferred_element_type=jnp.float32)  7.32 us
    ppermute x3, starting transfers between devices, follow_the_entries(): front.append(ppermute(front[-1], ax_name, rows))  5.68 us
  transfers between devices with their start and end apart: 9, of which 8 were waited for; matrix products, arithmetic and copies ran while one was open for 5% of the time, Pallas kernels for 0%

profile of v1, /device:TPU:0, one launch (start us, length us, event | category | flops | bytes accessed | tf_op | source)
XLA Modules:
  0.0 283.4 jit_solution(14175212747093213094)
XLA Ops:
  7.3 3.0 %collective-permute-start = (bf16[32,4096]{1,0:T(8,128)(2,1)}, bf16[32,4096]{1,0:T(8,128)(2,1)S(1)}, u32[]{:S(2)}, u32[]{:S(2)}) collective-permute-start(bf16[32,4096]{1,0:T(8,128)(2,1)} %param.7), channel_id=1, source_target_pairs={{0,2},{2,4},{4,6},{6,8},{8,10},{10,12},{12,14},{14,0},{1,3},{3,5},... | collective-permute-start | bytes 786440 | tf_op jit(solution)/shard_map/ppermute | solution.py:23
  10.3 9.6 %collective-permute-done = bf16[32,4096]{1,0:T(8,128)(2,1)S(1)} collective-permute-done((bf16[32,4096]{1,0:T(8,128)(2,1)}, bf16[32,4096]{1,0:T(8,128)(2,1)S(1)}, u32[]{:S(2)}, u32[]{:S(2)}) %collective-permute-start) | collective-permute-done | bytes 262176 | tf_op jit(solution)/shard_map/ppermute | solution.py:23
  19.9 4.7 %collective-permute-start.4 = (bf16[32,4096]{1,0:T(8,128)(2,1)}, bf16[32,4096]{1,0:T(8,128)(2,1)S(1)}, u32[]{:S(2)}, u32[]{:S(2)}) collective-permute-start(bf16[32,4096]{1,0:T(8,128)(2,1)} %param.7), channel_id=1, source_target_pairs={{0,14},{2,0},{4,2},{6,4},{8,6},{10,8},{12,10},{14,12},{1,15},{3,1}... | collective-permute-start | bytes 786440 | tf_op jit(solution)/shard_map/ppermute | solution.py:25
  24.6 11.7 %collective-permute-done.1 = bf16[32,4096]{1,0:T(8,128)(2,1)S(1)} collective-permute-done((bf16[32,4096]{1,0:T(8,128)(2,1)S(1)}, bf16[32,4096]{1,0:T(8,128)(2,1)S(1)}, u32[]{:S(2)}, u32[]{:S(2)}) %collective-permute-start.1) | collective-permute-done | bytes 262176 | tf_op jit(solution)/shard_map/ppermute | solution.py:23
  36.3 3.1 %collective-permute-start.2 = (bf16[32,4096]{1,0:T(8,128)(2,1)S(1)}, bf16[32,4096]{1,0:T(8,128)(2,1)S(1)}, u32[]{:S(2)}, u32[]{:S(2)}) collective-permute-start(bf16[32,4096]{1,0:T(8,128)(2,1)S(1)} %collective-permute-done.1), channel_id=1, source_target_pairs={{0,2},{2,4},{4,6},{6,8},{8,10},{10,12},{12,14},{14,0},{1,3},{3,5},... | collective-permute-start | bytes 786440 | tf_op jit(solution)/shard_map/ppermute | solution.py:23
  39.4 2.2 collective-permute-done.4
  41.6 12.8 %collective-permute-done.2 = bf16[32,4096]{1,0:T(8,128)(2,1)S(1)} collective-permute-done((bf16[32,4096]{1,0:T(8,128)(2,1)S(1)}, bf16[32,4096]{1,0:T(8,128)(2,1)S(1)}, u32[]{:S(2)}, u32[]{:S(2)}) %collective-permute-start.2) | collective-permute-done | bytes 262176 | tf_op jit(solution)/shard_map/ppermute | solution.py:23
  54.4 2.5 collective-permute-start.3
  60.1 8.9 %collective-permute-done.3 = bf16[32,4096]{1,0:T(8,128)(2,1)S(1)} collective-permute-done((bf16[32,4096]{1,0:T(8,128)(2,1)S(1)}, bf16[32,4096]{1,0:T(8,128)(2,1)S(1)}, u32[]{:S(2)}, u32[]{:S(2)}) %collective-permute-start.3) | collective-permute-done | bytes 262176 | tf_op jit(solution)/shard_map/ppermute | solution.py:23
  71.9 1.7 constant_dynamic-update-slice_fusion.11
  81.7 74.7 %all-gather.2.cloned.1.call-done = bf16[128,32768]{1,0:T(8,128)(2,1)} async-done(((bf16[128,4096]{1,0:T(8,128)(2,1)}), bf16[128,32768]{1,0:T(8,128)(2,1)}) %all-gather.2.cloned.1.call-update) | async-done | bytes 8388624 | tf_op jit(solution)/shard_map/all_gather | solution.py:32
  156.4 4.5 %multiply_reduce_fusion.3 = (f32[8192]{0:T(1024)S(1)}, f32[8192]{0:T(1024)S(1)}, f32[8192]{0:T(1024)S(1)}, f32[8192]{0:T(1024)S(1)}) fusion(bf16[128,32768]{1,0:T(8,128)(2,1)} %all-gather.2.cloned.1.call-done), kind=kLoop, calls=%fused_computation.28 | loop fusion | flops 12550144 | bytes 8519680 | tf_op jit(solution)/shard_map/reduce_sum | solution.py:9
  162.3 1.8 fusion.18
  164.1 2.5 fusion.28
  166.7 1.8 fusion.17
  168.5 2.5 fusion.30
  171.1 1.8 fusion.19
  172.9 2.5 fusion.26
  175.4 1.8 fusion.16
  177.3 2.1 fusion.25
  179.4 3.4 %psum.7 = f32[192,32]{0,1:T(8,128)S(1)} all-reduce(f32[192,32]{0,1:T(8,128)S(1)} %fusion.25), channel_id=1, replica_groups=mesh['grp'=2,'pts'=8,'ctr'=2] {'ctr'}, use_global_device_ids=true, to_apply=%region_5.6 | all-reduce | flops 6144 | bytes 49152 | tf_op jit(solution)/shard_map/psum | solution.py:46
  182.9 2.7 fusion.40
  188.0 2.2 pad_maximum_fusion
  190.3 86.3 %reduce-scatter.2.cloned.1.call-done = f32[32,4096]{1,0:T(8,128)} async-done(((f32[32,32768]{1,0:T(8,128)}), f32[32,4096]{1,0:T(8,128)}) %reduce-scatter.2.cloned.1.call-update) | async-done | bytes 524304 | tf_op jit(solution)/shard_map/reduce_scatter | solution.py:58
  (47 shorter events, 18.8 us)
Async XLA Ops:
  6.5 72.2 %copy-start.6 = (bf16[32,4096]{1,0:T(8,128)(2,1)S(1)}, bf16[32,4096]{1,0:T(8,128)(2,1)}, u32[]{:S(2)}) copy-start(bf16[32,4096]{1,0:T(8,128)(2,1)} %param.7) | copy-start | bytes 786436
  6.5 149.9 %all-gather.2.cloned.1.call-start = ((), (), s32[]{:S(2)}) async-start(), calls=%async_computation.1 | async-start | bytes 9437184 | tf_op jit(solution)/shard_map/all_gather | solution.py:32
  7.3 269.3 %reduce-scatter.2.cloned.1.call-start = ((), (), s32[]{:S(2)}) async-start(), calls=%async_computation.2 | async-start | bytes 4718592 | tf_op jit(solution)/shard_map/reduce_scatter | solution.py:58
  7.3 12.5 %collective-permute-start = (bf16[32,4096]{1,0:T(8,128)(2,1)}, bf16[32,4096]{1,0:T(8,128)(2,1)S(1)}, u32[]{:S(2)}, u32[]{:S(2)}) collective-permute-start(bf16[32,4096]{1,0:T(8,128)(2,1)} %param.7), channel_id=1, source_target_pairs={{0,2},{2,4},{4,6},{6,8},{8,10},{10,12},{12,14},{14,0},{1,3},{3,5},... | collective-permute-start | bytes 786440 | tf_op jit(solution)/shard_map/ppermute | solution.py:23
  19.9 16.4 %collective-permute-start.1 = (bf16[32,4096]{1,0:T(8,128)(2,1)S(1)}, bf16[32,4096]{1,0:T(8,128)(2,1)S(1)}, u32[]{:S(2)}, u32[]{:S(2)}) collective-permute-start(bf16[32,4096]{1,0:T(8,128)(2,1)S(1)} %collective-permute-done), channel_id=1, source_target_pairs={{0,2},{2,4},{4,6},{6,8},{8,10},{10,12},{12,14},{14,0},{1,3},{3,5},... | collective-permute-start | bytes 786440 | tf_op jit(solution)/shard_map/ppermute | solution.py:23
  19.9 21.7 %collective-permute-start.4 = (bf16[32,4096]{1,0:T(8,128)(2,1)}, bf16[32,4096]{1,0:T(8,128)(2,1)S(1)}, u32[]{:S(2)}, u32[]{:S(2)}) collective-permute-start(bf16[32,4096]{1,0:T(8,128)(2,1)} %param.7), channel_id=1, source_target_pairs={{0,14},{2,0},{4,2},{6,4},{8,6},{10,8},{12,10},{14,12},{1,15},{3,1}... | collective-permute-start | bytes 786440 | tf_op jit(solution)/shard_map/ppermute | solution.py:25
  36.3 18.1 %collective-permute-start.2 = (bf16[32,4096]{1,0:T(8,128)(2,1)S(1)}, bf16[32,4096]{1,0:T(8,128)(2,1)S(1)}, u32[]{:S(2)}, u32[]{:S(2)}) collective-permute-start(bf16[32,4096]{1,0:T(8,128)(2,1)S(1)} %collective-permute-done.1), channel_id=1, source_target_pairs={{0,2},{2,4},{4,6},{6,8},{8,10},{10,12},{12,14},{14,0},{1,3},{3,5},... | collective-permute-start | bytes 786440 | tf_op jit(solution)/shard_map/ppermute | solution.py:23
  41.6 17.6 %collective-permute-start.5 = (bf16[32,4096]{1,0:T(8,128)(2,1)S(1)}, bf16[32,4096]{1,0:T(8,128)(2,1)S(1)}, u32[]{:S(2)}, u32[]{:S(2)}) collective-permute-start(bf16[32,4096]{1,0:T(8,128)(2,1)S(1)} %collective-permute-done.4), channel_id=1, source_target_pairs={{0,14},{2,0},{4,2},{6,4},{8,6},{10,8},{12,10},{14,12},{1,15},{3,1}... | collective-permute-start | bytes 786440 | tf_op jit(solution)/shard_map/ppermute | solution.py:25
  54.4 14.6 %collective-permute-start.3 = (bf16[32,4096]{1,0:T(8,128)(2,1)S(1)}, bf16[32,4096]{1,0:T(8,128)(2,1)S(1)}, u32[]{:S(2)}, u32[]{:S(2)}) collective-permute-start(bf16[32,4096]{1,0:T(8,128)(2,1)S(1)} %collective-permute-done.2), channel_id=1, source_target_pairs={{0,2},{2,4},{4,6},{6,8},{8,10},{10,12},{12,14},{14,0},{1,3},{3,5},... | collective-permute-start | bytes 786440 | tf_op jit(solution)/shard_map/ppermute | solution.py:23
  59.2 15.9 %collective-permute-start.6 = (bf16[32,4096]{1,0:T(8,128)(2,1)S(1)}, bf16[32,4096]{1,0:T(8,128)(2,1)S(1)}, u32[]{:S(2)}, u32[]{:S(2)}) collective-permute-start(bf16[32,4096]{1,0:T(8,128)(2,1)S(1)} %collective-permute-done.5), channel_id=1, source_target_pairs={{0,14},{2,0},{4,2},{6,4},{8,6},{10,8},{12,10},{14,12},{1,15},{3,1}... | collective-permute-start | bytes 786440 | tf_op jit(solution)/shard_map/ppermute | solution.py:25
  81.7 79.3 %copy-start.7 = (bf16[192,128]{1,0:T(8,128)(2,1)S(1)}, bf16[192,128]{1,0:T(8,128)(2,1)}, u32[]{:S(2)}) copy-start(bf16[192,128]{1,0:T(8,128)(2,1)} %param.4) | copy-start | bytes 147460
  156.4 5.9 %copy-start.5 = (bf16[128,32768]{1,0:T(8,128)(2,1)S(1)}, bf16[128,32768]{1,0:T(8,128)(2,1)}, u32[]{:S(2)}) copy-start(bf16[128,32768]{1,0:T(8,128)(2,1)} %all-gather.2.cloned.1.call-done) | copy-start | bytes 25165828
  164.1 4.4 %copy-start = (bf16[192,8192]{1,0:T(8,128)(2,1)}, bf16[192,8192]{1,0:T(8,128)(2,1)S(1)}, u32[]{:S(2)}) copy-start(bf16[192,8192]{1,0:T(8,128)(2,1)S(1)} %fusion.18) | copy-start | bytes 9437188
  168.5 4.4 %copy-start.2 = (bf16[192,8192]{1,0:T(8,128)(2,1)}, bf16[192,8192]{1,0:T(8,128)(2,1)S(1)}, u32[]{:S(2)}) copy-start(bf16[192,8192]{1,0:T(8,128)(2,1)S(1)} %fusion.17) | copy-start | bytes 9437188
  172.9 4.4 %copy-start.4 = (bf16[192,8192]{1,0:T(8,128)(2,1)}, bf16[192,8192]{1,0:T(8,128)(2,1)S(1)}, u32[]{:S(2)}) copy-start(bf16[192,8192]{1,0:T(8,128)(2,1)S(1)} %fusion.19) | copy-start | bytes 9437188
  175.4 7.4 %copy-start.8 = (bf16[192,32]{0,1:T(8,128)(2,1)S(1)}, bf16[192,32]{0,1:T(8,128)(2,1)}, u32[]{:S(2)}) copy-start(bf16[192,32]{0,1:T(8,128)(2,1)} %param.5) | copy-start | bytes 36868
  182.9 2.8 %copy-start.1 = (bf16[192,8192]{1,0:T(8,128)(2,1)S(1)}, bf16[192,8192]{1,0:T(8,128)(2,1)}, u32[]{:S(2)}) copy-start(bf16[192,8192]{1,0:T(8,128)(2,1)} %copy-done) | copy-start | bytes 9437188
  182.9 3.8 %copy-start.3 = (bf16[192,8192]{1,0:T(8,128)(2,1)S(1)}, bf16[192,8192]{1,0:T(8,128)(2,1)}, u32[]{:S(2)}) copy-start(bf16[192,8192]{1,0:T(8,128)(2,1)} %copy-done.2) | copy-start | bytes 9437188
Sparse Core Ops, SparseCore 0:
  9.5 146.8 all-gather.1
  190.4 86.1 reduce-scatter.1
